TPU v7x, 128 devices: a whole 4x4x4 slice. The times are simulated.
128 devices in a mesh: rep: 8 (over x_lo, y), shard: 16 (over x_hi, z, core).
Axes of the slice: x: 4 (x_hi: 2, x_lo: 2; x = x_hi * 2 + x_lo), y: 4, z: 4, core: 2. Of those that a mesh axis runs over, the one named last changes fastest.
Arguments:
- tokens: bfloat16 [32768, 768], P(('rep', 'shard')), may hold values from -6 to 6
- segment_ids: int32 [8, 4096], P('rep'), may hold values from 0 to 15, never falling along the last dimension, each value on 1 to 2000 neighbouring positions
- norm1_gain: bfloat16 [768], P('shard'), may hold values from 0.099609375 to 1.8984375
- w_qkv: bfloat16 [768, 2304], P('shard'), may hold values from -0.21875 to 0.21875
- w_attn_out: bfloat16 [768, 768], P('shard'), may hold values from -1.25 to 1.25
- norm2_gain: bfloat16 [768], P('shard'), may hold values from 0.099609375 to 1.8984375
- w_in: bfloat16 [768, 2304], P('shard'), may hold values from -0.21875 to 0.21875
- w_mlp_out: bfloat16 [1152, 768], P('shard'), may hold values from -0.1875 to 0.1875
- cotangent: bfloat16 [32768, 768], P(('rep', 'shard')), may hold values from -24 to 24
Outputs:
- output: bfloat16 [32768, 768], P(('rep', 'shard'))
- grad_tokens: bfloat16 [32768, 768], P(('rep', 'shard'))
- grad_norm1_gain: float32 [768], P('shard')
- grad_w_qkv: float32 [768, 2304], P('shard')
- grad_w_attn_out: float32 [768, 768], P('shard')
- grad_norm2_gain: float32 [768], P('shard')
- grad_w_in: float32 [768, 2304], P('shard')
- grad_w_mlp_out: float32 [1152, 768], P('shard')
Inputs may be any that keep to these rules, and one draw needn't show every extreme that they name: `segment_ids`: along a sequence the ids never fall; each id from 0 to 15 is used by 1 to 2000 consecutive tokens, and one document has exactly 2000.
All inputs are finite; a program needn't handle non-finite values.
Results may differ from a plain program's by a relative error of at most 0.025.
Values may be sent and summed in bfloat16 or wider, within the bound.
No kernel may reach another device: no remote copies, remote signals or barrier semaphores. Data moves between devices by JAX's collectives and lax.ppermute only.
A program may use at most 128 MiB of HBM per device.

v0:
```python
import math

import jax
import jax.numpy as jnp
from jax import lax
from jax.sharding import PartitionSpec as P

HEADS = 12
HEAD = 64
HALF = 64


norm_epsilon = 1e-05
masked_score = -1e30
root_half = 0.7071067811865476
density_factor = 0.3989422804014327


def padded(cells, sides, width):
    for axis, dim in sides:
        count = lax.axis_size(axis)
        ends = count - 1
        head = lax.slice_in_dim(cells, 0, width, axis=dim)
        tail = lax.slice_in_dim(cells, cells.shape[dim] - width, cells.shape[dim], axis=dim)
        cells = jnp.concatenate(
            [
                lax.ppermute(tail, axis, [(i, (i + 1) % count) for i in range(ends)]),
                cells,
                lax.ppermute(head, axis, [((i + 1) % count, i) for i in range(ends)]),
            ],
            axis=dim,
        )
    return cells


def shifted(value, axis, steps):
    count = lax.axis_size(axis)
    leading, last = (max(0, -steps), min(count, count - steps))
    return lax.ppermute(value, axis, [(source, source + steps) for source in range(leading, last)])


def normalize_rows(values):
    centre = values - jnp.mean(values, axis=-1, keepdims=True)
    spread = jnp.mean(centre * centre, axis=-1, keepdims=True)
    row_inverse_scale = lax.rsqrt(spread + norm_epsilon)
    return (centre * row_inverse_scale, row_inverse_scale)


def norm_backward_pass(normalized_gradient, standardized_rows, row_inverse_scale):
    centered_average = jnp.mean(normalized_gradient, axis=-1, keepdims=True)
    projected_average = jnp.mean(normalized_gradient * standardized_rows, axis=-1, keepdims=True)
    return row_inverse_scale * (
        normalized_gradient - centered_average - standardized_rows * projected_average
    )


def rotate(vectors, cosine_table, sine_table):
    half_size = vectors.shape[-1] // 2
    turned = jnp.concatenate([-vectors[..., half_size:], vectors[..., :half_size]], axis=-1)
    return vectors * cosine_table + turned * sine_table


def rotate_back(vectors, cosine_table, sine_table):
    half_size = vectors.shape[-1] // 2
    scaled = vectors * sine_table
    turned = jnp.concatenate([scaled[..., half_size:], -scaled[..., :half_size]], axis=-1)
    return vectors * cosine_table + turned


def angles(position, head_width):
    fractions = jnp.arange(0, head_width, 2).astype(jnp.float32) / head_width
    inverse = jnp.exp(-math.log(10000.0) * fractions)
    phases = position.astype(jnp.float32)[:, None] * inverse[None, :]
    phases = jnp.concatenate([phases, phases], axis=-1)
    return (jnp.cos(phases)[:, None, :], jnp.sin(phases)[:, None, :])


def shards(
    tokens, segment_ids, norm1_gain, w_qkv, w_attn_out, norm2_gain, w_in, w_mlp_out, cotangent
):
    row_count = tokens.shape[0]
    model_width = tokens.shape[1]
    hidden_units = w_in.shape[1] // 2
    head_count = HEADS
    head_size = HEAD
    rim_width = HALF
    key_span = row_count + 2 * rim_width
    score_scale = 1.0 / math.sqrt(head_size)
    shard_place = lax.axis_index("shard")
    first_row = shard_place * row_count
    seq_segs = segment_ids[0]
    own_segs = lax.dynamic_slice_in_dim(seq_segs, first_row, row_count, 0)
    earlier = jnp.sum((seq_segs[None, :] < own_segs[:, None]).astype(jnp.int32), axis=1)
    position = jnp.arange(row_count, dtype=jnp.int32) + first_row - earlier
    cosine_table, sine_table = angles(position, head_size)
    segs_pad = jnp.pad(seq_segs, (rim_width, rim_width), constant_values=-1)
    key_segs = lax.dynamic_slice_in_dim(segs_pad, first_row, key_span, 0)
    row_index = jnp.arange(row_count, dtype=jnp.int32)[:, None] + rim_width
    column_index = jnp.arange(key_span, dtype=jnp.int32)[None, :]
    allowed = (jnp.abs(row_index - column_index) <= rim_width) & (
        own_segs[:, None] == key_segs[None, :]
    )
    input_rows = tokens.astype(jnp.float32)
    first_standardized, first_inverse_scale = normalize_rows(input_rows)
    gain_piece = lax.all_gather(norm1_gain, "shard", axis=0, tiled=True)
    weight_piece = lax.all_gather(w_qkv, "shard", axis=0, tiled=True)
    column_total = first_standardized
    normed_part = (column_total * gain_piece.astype(jnp.float32)).astype(jnp.bfloat16)
    qkv_all = jnp.dot(normed_part, weight_piece, preferred_element_type=jnp.float32)
    split_parts = qkv_all.reshape(row_count, 3, head_count, head_size)
    queries = rotate(split_parts[:, 0], cosine_table, sine_table).astype(jnp.bfloat16)
    key_rows = rotate(split_parts[:, 1], cosine_table, sine_table).astype(jnp.bfloat16)
    values = split_parts[:, 2].astype(jnp.bfloat16)
    joined = jnp.concatenate(
        [key_rows.reshape(row_count, model_width), values.reshape(row_count, model_width)], axis=1
    )
    joined_ext = padded(joined, (("shard", 0),), rim_width)
    keys_ext = joined_ext[:, :model_width].reshape(key_span, head_count, head_size)
    values_ext = joined_ext[:, model_width:].reshape(key_span, head_count, head_size)

    def scores_of():
        raw_scores = (
            jnp.einsum("qhd,khd->hqk", queries, keys_ext, preferred_element_type=jnp.float32)
            * score_scale
        )
        return jnp.where(allowed[None], raw_scores, masked_score)

    scores = scores_of()
    row_max = jnp.max(scores, axis=-1, keepdims=True)
    exponent = jnp.exp(scores - row_max)
    row_total = jnp.sum(exponent, axis=-1, keepdims=True)
    log_total = row_max + jnp.log(row_total)
    probs_low = (exponent / row_total).astype(jnp.bfloat16)
    context = jnp.einsum("hqk,khd->qhd", probs_low, values_ext, preferred_element_type=jnp.float32)
    context = context.reshape(row_count, model_width).astype(jnp.bfloat16)
    column_total = context
    attn_out = jnp.dot(
        column_total,
        lax.all_gather(w_attn_out, "shard", axis=0, tiled=True),
        preferred_element_type=jnp.float32,
    )
    hidden_rows = input_rows + attn_out
    second_standardized, second_inverse_scale = normalize_rows(hidden_rows)
    gain_piece = lax.all_gather(norm2_gain, "shard", axis=0, tiled=True)
    weight_piece = lax.all_gather(w_in, "shard", axis=0, tiled=True)
    column_total = second_standardized
    normed_part = (column_total * gain_piece.astype(jnp.float32)).astype(jnp.bfloat16)
    gate_up = jnp.dot(normed_part, weight_piece, preferred_element_type=jnp.float32)
    gate_part = gate_up[:, :hidden_units]
    up_part = gate_up[:, hidden_units:]
    activated = jax.nn.gelu(gate_part, approximate=False)
    mixed_rows = (activated * up_part).astype(jnp.bfloat16)
    column_total = mixed_rows
    mlp_out = jnp.dot(
        column_total,
        lax.all_gather(w_mlp_out, "shard", axis=0, tiled=True),
        preferred_element_type=jnp.float32,
    )
    output = (hidden_rows + mlp_out).astype(jnp.bfloat16)
    grad_out = cotangent.astype(jnp.float32)
    second_norm_gains, win_all, wdown_all = (
        lax.all_gather(norm2_gain, "shard", axis=0, tiled=True),
        lax.all_gather(w_in, "shard", axis=0, tiled=True),
        lax.all_gather(w_mlp_out, "shard", axis=0, tiled=True),
    )
    second_normalized = (second_standardized * second_norm_gains.astype(jnp.float32)).astype(
        jnp.bfloat16
    )
    term_down = jnp.einsum("tf,td->fd", mixed_rows, cotangent, preferred_element_type=jnp.float32)
    grad_mixed = jnp.einsum("td,fd->tf", cotangent, wdown_all, preferred_element_type=jnp.float32)
    normal_cdf = 0.5 * (1.0 + lax.erf(gate_part * root_half))
    normal_pdf = jnp.exp(-0.5 * gate_part * gate_part) * density_factor
    grad_gate = grad_mixed * up_part * (normal_cdf + gate_part * normal_pdf)
    grad_up = grad_mixed * activated
    grad_gate_up = jnp.concatenate([grad_gate, grad_up], axis=1).astype(jnp.bfloat16)
    term_in = jnp.einsum(
        "td,tf->df", second_normalized, grad_gate_up, preferred_element_type=jnp.float32
    )
    second_normalized_gradient = jnp.einsum(
        "tf,df->td", grad_gate_up, win_all, preferred_element_type=jnp.float32
    )
    second_gain_term = jnp.sum(second_normalized_gradient * second_standardized, axis=0)
    hidden_gradient = grad_out + norm_backward_pass(
        second_normalized_gradient * second_norm_gains.astype(jnp.float32),
        second_standardized,
        second_inverse_scale,
    )
    mlp_parts = (
        lax.psum_scatter(
            second_gain_term.astype(jnp.bfloat16), "shard", scatter_dimension=0, tiled=True
        ).astype(jnp.float32),
        lax.psum_scatter(
            term_in.astype(jnp.bfloat16), "shard", scatter_dimension=0, tiled=True
        ).astype(jnp.float32),
        lax.psum_scatter(
            term_down.astype(jnp.bfloat16), "shard", scatter_dimension=0, tiled=True
        ).astype(jnp.float32),
    )
    first_norm_gains, wqkv_all, wout_all = (
        lax.all_gather(norm1_gain, "shard", axis=0, tiled=True),
        lax.all_gather(w_qkv, "shard", axis=0, tiled=True),
        lax.all_gather(w_attn_out, "shard", axis=0, tiled=True),
    )
    first_normalized = (first_standardized * first_norm_gains.astype(jnp.float32)).astype(
        jnp.bfloat16
    )
    grad_attn = hidden_gradient.astype(jnp.bfloat16)
    term_out = jnp.einsum("td,te->de", context, grad_attn, preferred_element_type=jnp.float32)
    grad_context = jnp.einsum("te,de->td", grad_attn, wout_all, preferred_element_type=jnp.float32)
    grad_context = grad_context.astype(jnp.bfloat16).reshape(row_count, head_count, head_size)
    attn_probs = jnp.exp(scores_of() - log_total)
    probs_again = attn_probs.astype(jnp.bfloat16)
    grad_probs = jnp.einsum(
        "qhd,khd->hqk", grad_context, values_ext, preferred_element_type=jnp.float32
    )
    inner = jnp.sum(attn_probs * grad_probs, axis=-1, keepdims=True)
    grad_scores = (attn_probs * (grad_probs - inner)).astype(jnp.bfloat16)
    grad_queries = (
        jnp.einsum("hqk,khd->qhd", grad_scores, keys_ext, preferred_element_type=jnp.float32)
        * score_scale
    )
    grad_keys_ext = (
        jnp.einsum("hqk,qhd->khd", grad_scores, queries, preferred_element_type=jnp.float32)
        * score_scale
    )
    grad_values_ext = jnp.einsum(
        "hqk,qhd->khd", probs_again, grad_context, preferred_element_type=jnp.float32
    )
    grad_joined = jnp.concatenate(
        [
            grad_keys_ext.reshape(key_span, model_width),
            grad_values_ext.reshape(key_span, model_width),
        ],
        axis=1,
    )
    from_below = shifted(
        grad_joined[row_count + rim_width :].astype(jnp.bfloat16), "shard", 1
    ).astype(jnp.float32)
    from_above = shifted(grad_joined[:rim_width].astype(jnp.bfloat16), "shard", -1).astype(
        jnp.float32
    )
    own_grads = grad_joined[rim_width : rim_width + row_count]
    own_grads = own_grads.at[:rim_width].add(from_below)
    own_grads = own_grads.at[row_count - rim_width :].add(from_above)
    grad_keys = own_grads[:, :model_width].reshape(row_count, head_count, head_size)
    grad_values = own_grads[:, model_width:]
    grad_qkv = jnp.concatenate(
        [
            rotate_back(grad_queries, cosine_table, sine_table).reshape(row_count, model_width),
            rotate_back(grad_keys, cosine_table, sine_table).reshape(row_count, model_width),
            grad_values,
        ],
        axis=1,
    ).astype(jnp.bfloat16)
    term_qkv = jnp.einsum(
        "td,te->de", first_normalized, grad_qkv, preferred_element_type=jnp.float32
    )
    first_normalized_gradient = jnp.einsum(
        "te,de->td", grad_qkv, wqkv_all, preferred_element_type=jnp.float32
    )
    first_gain_term = jnp.sum(first_normalized_gradient * first_standardized, axis=0)
    grad_tokens = (
        hidden_gradient
        + norm_backward_pass(
            first_normalized_gradient * first_norm_gains.astype(jnp.float32),
            first_standardized,
            first_inverse_scale,
        )
    ).astype(jnp.bfloat16)
    attn_parts = (
        lax.psum_scatter(
            first_gain_term.astype(jnp.bfloat16), "shard", scatter_dimension=0, tiled=True
        ).astype(jnp.float32),
        lax.psum_scatter(
            term_qkv.astype(jnp.bfloat16), "shard", scatter_dimension=0, tiled=True
        ).astype(jnp.float32),
        lax.psum_scatter(
            term_out.astype(jnp.bfloat16), "shard", scatter_dimension=0, tiled=True
        ).astype(jnp.float32),
    )
    summed = (
        lax.psum(attn_parts[0].astype(jnp.bfloat16), "rep").astype(jnp.float32),
        lax.psum(attn_parts[1].astype(jnp.bfloat16), "rep").astype(jnp.float32),
        lax.psum(attn_parts[2].astype(jnp.bfloat16), "rep").astype(jnp.float32),
        lax.psum(mlp_parts[0].astype(jnp.bfloat16), "rep").astype(jnp.float32),
        lax.psum(mlp_parts[1].astype(jnp.bfloat16), "rep").astype(jnp.float32),
        lax.psum(mlp_parts[2].astype(jnp.bfloat16), "rep").astype(jnp.float32),
    )
    return (output, grad_tokens, summed[0], summed[1], summed[2], summed[3], summed[4], summed[5])


def solution(mesh):
    return jax.shard_map(
        shards,
        mesh=mesh,
        in_specs=(
            P(("rep", "shard"), None),
            P("rep", None),
            P("shard"),
            P("shard", None),
            P("shard", None),
            P("shard"),
            P("shard", None),
            P("shard", None),
            P(("rep", "shard"), None),
        ),
        out_specs=(
            P(("rep", "shard"), None),
            P(("rep", "shard"), None),
            P("shard"),
            P("shard", None),
            P("shard", None),
            P("shard"),
            P("shard", None),
            P("shard", None),
        ),
        check_vma=False,
    )
```

profile of v0, /device:TPU:0, one launch (start us, length us, event | category | flops | bytes accessed | tf_op | source)
XLA Modules:
  0.0 613.6 jit_solution(3738105893243171046)
XLA Ops:
  13.8 39.4 %all-reduce.6 = (bf16[768]{0:T(1024)(128)(2,1)S(1)}, bf16[768]{0:T(1024)(128)(2,1)S(1)}) all-reduce(bf16[768]{0:T(1024)(128)(2,1)S(1)} %dynamic-update-slice.6, bf16[768]{0:T(1024)(128)(2,1)S(1)} %dynamic-update-slice.7), channel_id=1, replica_groups=mesh['rep'=8,'shard'=16] {'shard'}, use_global_device_ids=true, to_apply=%add.1 | all-reduce | flops 1536 | bytes 6144
  56.1 9.5 %all-gather.5.cloned.1.call-done = bf16[768,2304]{1,0:T(8,128)(2,1)} async-done(((bf16[48,2304]{1,0:T(8,128)(2,1)}), bf16[768,2304]{1,0:T(8,128)(2,1)}) %all-gather.5.cloned.1.call-update) | async-done | bytes 3538960 | tf_op jit(solution)/shard_map/all_gather | solution.py:106
  65.6 3.6 fusion.61
  71.6 3.2 collective-permute-start
  81.7 32.6 %all-gather.7.cloned.1.call-done = bf16[768,768]{1,0:T(8,128)(2,1)} async-done(((bf16[48,768]{1,0:T(8,128)(2,1)}), bf16[768,768]{1,0:T(8,128)(2,1)}) %all-gather.7.cloned.1.call-update) | async-done | bytes 1179664 | tf_op jit(solution)/shard_map/all_gather | solution.py:139
  116.4 51.7 %all-gather.9.cloned.1.call-done = bf16[768,2304]{1,0:T(8,128)(2,1)} async-done(((bf16[48,2304]{1,0:T(8,128)(2,1)}), bf16[768,2304]{1,0:T(8,128)(2,1)}) %all-gather.9.cloned.1.call-update) | async-done | bytes 3538960 | tf_op jit(solution)/shard_map/all_gather | solution.py:145
  168.0 4.6 fusion.63
  172.6 42.6 %all-gather.11.cloned.1.call-done = bf16[1152,768]{1,0:T(8,128)(2,1)} async-done(((bf16[72,768]{1,0:T(8,128)(2,1)}), bf16[1152,768]{1,0:T(8,128)(2,1)}) %all-gather.11.cloned.1.call-update) | async-done | bytes 1769488 | tf_op jit(solution)/shard_map/all_gather | solution.py:156
  215.3 6.5 %multiply_convert_fusion.1 = (bf16[256,1152]{1,0:T(8,128)(2,1)S(1)}, f32[256,1152]{1,0:T(8,128)}, bf16[256,1152]{1,0:T(8,128)(2,1)S(1)}) fusion(f32[256,2304]{1,0:T(8,128)} %fusion.63, bf16[256,768]{1,0:T(8,128)(2,1)S(1)} %copy-done.7, bf16[1152,768]{1,0:T(8,128)(2,1)} %all-gather.11.cloned.1.call-done), kind=kOutput, calls=%fused_computation.47 | convolution fusion | flops 475693056 | bytes 6881280 | tf_op jit(solution)/shard_map/td,fd->tf/dot_general | solution.py:170
  229.7 2.5 convolution_convert_fusion.4
  233.4 4.3 convolution_convert_fusion
  238.1 3.8 multiply_reduce_fusion
  246.1 2.2 collective-permute-start.2
  253.4 6.6 %scatter-add.6 = f32[256,1536]{0,1:T(8,128)S(1)} dynamic-update-slice(f32[256,1536]{0,1:T(8,128)S(1)} %fusion.7, f32[64,1536]{0,1:T(8,128)} %fusion.44, s32[]{:T(128)} %constant.123.clone.1, s32[]{:T(128)} %constant.123.clone.1) | dynamic-update-slice | bytes 786436 | tf_op jit(solution)/shard_map/scatter-add | solution.py:243
  262.3 6.5 %scatter-add.9 = f32[256,1536]{0,1:T(8,128)S(1)} dynamic-update-slice(f32[256,1536]{0,1:T(8,128)S(1)} %scatter-add.6, f32[64,1536]{0,1:T(8,128)} %slice_add_fusion, s32[]{:T(128)} %constant.164.clone.1, s32[]{:T(128)} %constant.123.clone.1) | dynamic-update-slice | bytes 786436 | tf_op jit(solution)/shard_map/scatter-add | solution.py:244
  271.6 3.0 convolution_convert_fusion.1
  275.8 3.0 fusion.8
  278.8 2.3 fusion.37
  281.1 37.1 %all-reduce.5 = (bf16[768]{0:T(1024)(128)(2,1)S(1)}, bf16[768]{0:T(1024)(128)(2,1)S(1)}) all-reduce(bf16[768]{0:T(1024)(128)(2,1)S(1)} %get-tuple-element.34, bf16[768]{0:T(1024)(128)(2,1)S(1)} %get-tuple-element.32), channel_id=2, replica_groups=mesh['rep'=8,'shard'=16] {'shard'}, use_global_device_ids=true, to_apply=%region_13.14.clone | all-reduce | flops 1536 | bytes 6144
  318.4 19.6 %all-reduce.7 = (bf16[48]{0:T(256)(128)(2,1)S(1)}, bf16[48]{0:T(256)(128)(2,1)S(1)}) all-reduce(bf16[48]{0:T(256)(128)(2,1)S(1)} %dynamic-slice.20, bf16[48]{0:T(256)(128)(2,1)S(1)} %dynamic-slice.22), channel_id=1, replica_groups=mesh['rep'=8,'shard'=16] {'rep'}, use_global_device_ids=true, to_apply=%region_14.15 | all-reduce | flops 96 | bytes 384 | tf_op jit(solution)/shard_map/psum | solution.py:282
  339.0 24.9 %reduce-scatter.11.cloned.1.call-done = bf16[72,768]{1,0:T(8,128)(2,1)} async-done(((bf16[1152,768]{1,0:T(8,128)(2,1)}), bf16[72,768]{1,0:T(8,128)(2,1)}) %reduce-scatter.11.cloned.1.call-update) | async-done | bytes 110608 | tf_op jit(solution)/shard_map/reduce_scatter | solution.py:195
  363.9 80.3 %reduce-scatter.9.cloned.1.call-done = bf16[48,2304]{1,0:T(8,128)(2,1)} async-done(((bf16[768,2304]{1,0:T(8,128)(2,1)}), bf16[48,2304]{1,0:T(8,128)(2,1)}) %reduce-scatter.9.cloned.1.call-update) | async-done | bytes 221200 | tf_op jit(solution)/shard_map/reduce_scatter | solution.py:192
  444.2 80.1 %reduce-scatter.5.cloned.1.call-done = bf16[48,2304]{1,0:T(8,128)(2,1)} async-done(((bf16[768,2304]{1,0:T(8,128)(2,1)}), bf16[48,2304]{1,0:T(8,128)(2,1)}) %reduce-scatter.5.cloned.1.call-update) | async-done | bytes 221200 | tf_op jit(solution)/shard_map/reduce_scatter | solution.py:274
  525.4 76.0 %all-reduce.11.cloned.1.call-done = (bf16[48,2304]{1,0:T(8,128)(2,1)}, bf16[48,768]{1,0:T(8,128)(2,1)}, bf16[48,2304]{1,0:T(8,128)(2,1)}, bf16[72,768]{1,0:T(8,128)(2,1)}) async-done(((bf16[48,2304]{1,0:T(8,128)(2,1)}, bf16[48,768]{1,0:T(8,128)(2,1)}, bf16[48,2304]{1,0:T(8,128)(2,1)}, bf16[72,768]{1,0:T(8,128)(2,1)}), (bf16[48,2304]{1,0:T(8,128)(2,1)}, bf16[48,768]{1,0:T(8,128)(2,1)}, ...) | async-done | bytes 626704 | tf_op jit(solution)/shard_map/psum | solution.py:283
  (150 shorter events, 51.8 us)
Async XLA Ops:
  7.2 47.2 %copy-start.1 = (bf16[256,768]{1,0:T(8,128)(2,1)S(1)}, bf16[256,768]{1,0:T(8,128)(2,1)}, u32[]{:S(2)}) copy-start(bf16[256,768]{1,0:T(8,128)(2,1)} %param.13) | copy-start | bytes 1179652
  7.2 47.4 %copy-start.23 = (s32[1,4096]{1,0:T(1,128)S(1)}, s32[1,4096]{1,0:T(1,128)}, u32[]{:S(2)}) copy-start(s32[1,4096]{1,0:T(1,128)} %param.14) | copy-start | bytes 49156
  7.2 58.4 %all-gather.5.cloned.1.call-start = ((), (), s32[]{:S(2)}) async-start(), calls=%async_computation.4 | async-start | bytes 3760128 | tf_op jit(solution)/shard_map/all_gather | solution.py:106
  7.9 106.3 %all-gather.7.cloned.1.call-start = ((), (), s32[]{:S(2)}) async-start(), calls=%async_computation.5 | async-start | bytes 1253376 | tf_op jit(solution)/shard_map/all_gather | solution.py:139
  8.7 159.4 %all-gather.9.cloned.1.call-start = ((), (), s32[]{:S(2)}) async-start(), calls=%async_computation.6 | async-start | bytes 3760128 | tf_op jit(solution)/shard_map/all_gather | solution.py:145
  9.4 205.9 %all-gather.11.cloned.1.call-start = ((), (), s32[]{:S(2)}) async-start(), calls=%async_computation.7 | async-start | bytes 1880064 | tf_op jit(solution)/shard_map/all_gather | solution.py:156
  10.0 329.0 %reduce-scatter.7.cloned.1.call-start = ((), (), s32[]{:S(2)}) async-start(), calls=%async_computation.9 | async-start | bytes 1253376 | tf_op jit(solution)/shard_map/reduce_scatter | solution.py:277
  56.0 13.7 %copy-start.12 = (f32[256,64]{0,1:T(8,128)}, f32[256,64]{0,1:T(8,128)S(1)}, u32[]{:S(2)}) copy-start(f32[256,64]{0,1:T(8,128)S(1)} %get-tuple-element.72) | copy-start | bytes 196612
  56.0 13.9 %copy-start.10 = (f32[256,64]{0,1:T(8,128)}, f32[256,64]{0,1:T(8,128)S(1)}, u32[]{:S(2)}) copy-start(f32[256,64]{0,1:T(8,128)S(1)} %get-tuple-element.73) | copy-start | bytes 196612
  70.3 4.8 collective-permute-start.1
  71.6 4.4 collective-permute-start
  116.4 98.9 %copy-start.7 = (bf16[256,768]{1,0:T(8,128)(2,1)S(1)}, bf16[256,768]{1,0:T(8,128)(2,1)}, u32[]{:S(2)}) copy-start(bf16[256,768]{1,0:T(8,128)(2,1)} %param.21) | copy-start | bytes 1179652
  215.3 6.5 %copy-start.5 = (bf16[768,2304]{1,0:T(8,128)(2,1)S(1)}, bf16[768,2304]{1,0:T(8,128)(2,1)}, u32[]{:S(2)}) copy-start(bf16[768,2304]{1,0:T(8,128)(2,1)} %all-gather.9.cloned.1.call-done) | copy-start | bytes 10616836
  225.0 138.9 %reduce-scatter.11.cloned.1.call-start = ((), (), s32[]{:S(2)}) async-start(), calls=%async_computation.11 | async-start | bytes 1880064 | tf_op jit(solution)/shard_map/reduce_scatter | solution.py:195
  229.7 214.6 %reduce-scatter.9.cloned.1.call-start = ((), (), s32[]{:S(2)}) async-start(), calls=%async_computation.10 | async-start | bytes 3760128 | tf_op jit(solution)/shard_map/reduce_scatter | solution.py:192
  237.8 286.5 %reduce-scatter.5.cloned.1.call-start = ((), (), s32[]{:S(2)}) async-start(), calls=%async_computation.8 | async-start | bytes 3760128 | tf_op jit(solution)/shard_map/reduce_scatter | solution.py:274
  238.0 3.9 slice-start
  238.0 4.1 slice-start.1
  246.1 6.2 %collective-permute-start.2 = (bf16[64,1536]{0,1:T(8,128)(2,1)S(1)}, bf16[64,1536]{0,1:T(8,128)(2,1)S(1)}, u32[]{:S(2)}, u32[]{:S(2)}) collective-permute-start(bf16[64,1536]{0,1:T(8,128)(2,1)S(1)} %get-tuple-element.55), channel_id=1, source_target_pairs={{0,1},{1,2},{2,3},{3,4},{4,5},{5,6},{6,7},{7,8},{8,9},{9,10},{10,1... | collective-permute-start | bytes 589832 | tf_op jit(solution)/shard_map/ppermute | solution.py:39
  248.3 11.8 %collective-permute-start.3 = (bf16[64,1536]{0,1:T(8,128)(2,1)}, bf16[64,1536]{0,1:T(8,128)(2,1)}, u32[]{:S(2)}, u32[]{:S(2)}) collective-permute-start(bf16[64,1536]{0,1:T(8,128)(2,1)} %get-tuple-element.54), channel_id=1, source_target_pairs={{1,0},{2,1},{3,2},{4,3},{5,4},{6,5},{7,6},{8,7},{9,8},{10,9},{11,1... | collective-permute-start | bytes 589832 | tf_op jit(solution)/shard_map/ppermute | solution.py:39
  274.7 4.1 copy-start.17
  274.7 4.1 copy-start.19
  274.7 326.7 %all-reduce.11.cloned.1.call-start = ((), (), s32[]{:S(2)}) async-start(), calls=%async_computation.12 | async-start | bytes 1253376 | tf_op jit(solution)/shard_map/psum | solution.py:283
  601.4 5.0 copy-start.22
  (15 other events, 22.3 us)
Sparse Core Ops, SparseCore 0:
  10.5 55.0 all-gather.4
  68.1 46.1 all-gather.6
  116.8 51.2 all-gather.8
  170.3 44.9 all-gather.10
  225.1 66.3 reduce-scatter.6
  295.4 68.4 reduce-scatter.10
  368.0 76.1 reduce-scatter.8
  448.3 75.9 reduce-scatter.4
  527.1 74.2 all-reduce.10
where the time goes:
time: 615 us; the launch traced here: 614 us
  waiting for transfers between devices  401 us (65%)
  blocking collectives  96.1 us (16%)
  matrix products  45.8 us (7%)
  local copies, waits for them, and re-layouts  23.9 us (4%)
  other arithmetic  22.2 us (4%)
  between operations  15.9 us (3%)
  starting transfers between devices  8.58 us (1%)
    reduce_scatter x1, waiting for transfers between devices, shards(): lax.psum_scatter(term_in.astype(jnp.bfloat16), 'shard', scatter_dimension...  80.3 us
    reduce_scatter x1, waiting for transfers between devices, shards(): lax.psum_scatter(term_qkv.astype(jnp.bfloat16), 'shard', scatter_dimensio...  80.1 us
    unnamed x2, blocking collectives  76.5 us
    psum x1, waiting for transfers between devices, shards(): lax.psum(attn_parts[1].astype(jnp.bfloat16), 'rep').astype(jnp.float32)  76 us
    all_gather x1, waiting for transfers between devices, shards(): weight_piece = lax.all_gather(w_in, 'shard', axis=0, tiled=True)  51.7 us
    all_gather x1, waiting for transfers between devices, shards(): lax.all_gather(w_mlp_out, 'shard', axis=0, tiled=True)  42.6 us
    all_gather x1, waiting for transfers between devices, shards(): lax.all_gather(w_attn_out, 'shard', axis=0, tiled=True)  32.6 us
    reduce_scatter x1, waiting for transfers between devices, shards(): lax.psum_scatter(term_down.astype(jnp.bfloat16), 'shard', scatter_dimensi...  24.9 us
  transfers between devices with their start and end apart: 13, of which 9 were waited for; matrix products, arithmetic and copies ran while one was open for 12% of the time, Pallas kernels for 0%

commit v1 on v0

v1 whole, which is shorter than its diff:
```python
import math

import jax
import jax.numpy as jnp
from jax import lax
from jax.experimental import pallas as pl
from jax.experimental.pallas import tpu as pltpu
from jax.sharding import PartitionSpec as P

HEADS = 12
HEAD = 64
HALF = 64
WIDTH = 768
AXES = ("rep", "shard")
BF = jnp.bfloat16
F32 = jnp.float32

norm_epsilon = 1e-05
masked_score = -1e30
root_half = 0.7071067811865476
density_factor = 0.3989422804014327


def coordinates(device):
    rep, shard = divmod(device, 16)
    x_low, y = divmod(rep, 4)
    x_high, rest = divmod(shard, 8)
    z, core = divmod(rest, 2)
    return x_high * 2 + x_low, y, z, core


def number(x, y, z, core):
    return ((x % 2) * 4 + y) * 16 + (x // 2) * 8 + z * 2 + core


def pairs(move):
    return [(device, number(*move(*coordinates(device)))) for device in range(128)]


def along_z(step):
    return pairs(lambda x, y, z, core: (x, y, (z + step) % 4, core))


def along_y(step):
    return pairs(lambda x, y, z, core: (x, (y + step) % 4, z, core))


OTHER_CORE = pairs(lambda x, y, z, core: (x, y, z, 1 - core))
ACROSS_X = pairs(lambda x, y, z, core: (3 - x, y, z, core))
TWIN_X = pairs(lambda x, y, z, core: (x ^ 1, y, z, core))
Z_STEP = {step: along_z(step) for step in (1, 2, 3)}
Y_STEP = {step: along_y(step) for step in (1, 2, 3)}


def send(value, route):
    return lax.ppermute(value, AXES, route)


def place():
    shard = lax.axis_index("shard")
    rep = lax.axis_index("rep")
    return {
        "x_high": shard // 8,
        "z": (shard // 2) % 4,
        "core": shard % 2,
        "x_low": rep // 4,
        "y": rep % 4,
        "shard": shard,
    }


PIECES = [(0, 0), (1, 0), (0, 3), (0, 1), (0, 2), (1, 3), (1, 1), (1, 2)]


def gather_group(piece):
    own = {(0, 0): piece}
    own[1, 0] = send(piece, ACROSS_X)
    own[0, 3] = send(piece, Z_STEP[1])
    own[0, 1] = send(piece, Z_STEP[3])
    own[0, 2] = send(piece, Z_STEP[2])
    own[1, 3] = send(own[1, 0], Z_STEP[1])
    own[1, 1] = send(own[1, 0], Z_STEP[3])
    own[1, 2] = send(own[0, 2], ACROSS_X)
    mine = [own[key] for key in PIECES]
    return mine + [send(value, OTHER_CORE) for value in mine]


def row_blocks(where_ref):
    x_high, z, core = where_ref[0], where_ref[1], where_ref[2]
    blocks = []
    for turned, step in PIECES:
        side = 1 - x_high if turned else x_high
        blocks.append((side * 4 + lax.rem(z + step, 4)) * 2)
    return [b + core for b in blocks] + [b + 1 - core for b in blocks]


def at_rows(block, count):
    return pl.ds(pl.multiple_of(block * count, 16), count)


def assemble_first(where_ref, *refs):
    pieces, (weight_ref, gain_ref) = refs[:16], refs[16:]
    total = jnp.zeros((16, WIDTH), F32)
    for block, piece in zip(row_blocks(where_ref), pieces):
        for part in range(3):
            weight_ref[at_rows(block, 48), part * WIDTH : (part + 1) * WIDTH] = piece[
                part * 48 : (part + 1) * 48, :
            ]
        total = total + piece[144:160, :].astype(F32)
    gain_ref[...] = total


def assemble_second(where_ref, *refs):
    pieces, (out_ref, in_ref, down_ref) = refs[:16], refs[16:]
    blocks = row_blocks(where_ref)
    for block, piece in zip(blocks, pieces):
        out_ref[at_rows(block, 48), :] = piece[0:48, :]
        for part in range(3):
            in_ref[at_rows(block, 48), part * WIDTH : (part + 1) * WIDTH] = piece[
                (part + 1) * 48 : (part + 2) * 48, :
            ]
    core = where_ref[2]
    for mine, other, block in zip(pieces[:8], pieces[8:], blocks[:8]):
        here = mine[192:272, :].astype(F32)[:72]
        there = other[192:272, :].astype(F32)[:72]
        first = jnp.where(core == 0, here, there)
        second = jnp.where(core == 0, there, here)
        down_ref[at_rows(block // 2, 144), :] = jnp.concatenate([first, second], axis=0).astype(BF)


def whole_in_vmem(count):
    return [pl.BlockSpec(memory_space=pltpu.VMEM) for _ in range(count)]


def call(kernel, where, arrays, outs):
    return pl.pallas_call(
        kernel,
        out_shape=[jax.ShapeDtypeStruct(shape, kind) for shape, kind in outs],
        in_specs=[pl.BlockSpec(memory_space=pltpu.SMEM)] + whole_in_vmem(len(arrays)),
        out_specs=whole_in_vmem(len(outs)),
        compiler_params=pltpu.CompilerParams(vmem_limit_bytes=48 * 1024 * 1024),
    )(where, *arrays)


def take(values, index, axis):
    return lax.dynamic_index_in_dim(values, index, axis=axis, keepdims=False)


def core_sum(term, at, rows):
    split = term.reshape(8, 2, rows, WIDTH)
    arrived = send(take(split, 1 - at["core"], 1), OTHER_CORE)
    mine = take(split, at["core"], 1)
    return (mine.astype(F32) + arrived.astype(F32)).astype(BF).reshape(2, 4, rows, WIDTH)


def z_sum(blocks, at, axis):
    arrived = [send(take(blocks, (at["z"] + step) % 4, axis), Z_STEP[step]) for step in (1, 3, 2)]
    total = take(blocks, at["z"], axis).astype(F32)
    for value in arrived:
        total = total + value.astype(F32)
    return total.astype(BF)


def x_sum(blocks, at):
    arrived = send(take(blocks, 1 - at["x_high"], 0), ACROSS_X)
    return (take(blocks, at["x_high"], 0).astype(F32) + arrived.astype(F32)).astype(BF)


def shard_sum(blocks, at, cut):
    z_first = x_sum(z_sum(blocks[:, :, :cut], at, 1), at)
    x_first = z_sum(x_sum(blocks[:, :, cut:], at), at, 0)
    return jnp.concatenate([z_first, x_first], axis=0)


def rep_sum(block, at):
    rows = block.shape[0] // 4
    parts = block.reshape(4, rows, WIDTH)
    arrived = [send(take(parts, (at["y"] + step) % 4, 0), Y_STEP[step]) for step in (1, 3, 2)]
    total = take(parts, at["y"], 0).astype(F32)
    for value in arrived:
        total = total + value.astype(F32)
    total = total.astype(BF)
    total = (total.astype(F32) + send(total, TWIN_X).astype(F32)).astype(BF)
    ring = [total] + [send(total, Y_STEP[4 - step]) for step in (1, 2, 3)]
    ring = jnp.stack(ring + ring[:3])
    ordered = lax.dynamic_slice_in_dim(ring, (4 - at["y"]) % 4, 4, axis=0)
    return ordered.reshape(4 * rows, WIDTH)


def normalize_rows(values):
    centre = values - jnp.mean(values, axis=-1, keepdims=True)
    spread = jnp.mean(centre * centre, axis=-1, keepdims=True)
    row_inverse_scale = lax.rsqrt(spread + norm_epsilon)
    return (centre * row_inverse_scale, row_inverse_scale)


def norm_backward_pass(normalized_gradient, standardized_rows, row_inverse_scale):
    centered_average = jnp.mean(normalized_gradient, axis=-1, keepdims=True)
    projected_average = jnp.mean(normalized_gradient * standardized_rows, axis=-1, keepdims=True)
    return row_inverse_scale * (
        normalized_gradient - centered_average - standardized_rows * projected_average
    )


def rotate(vectors, cosine_table, sine_table):
    half_size = vectors.shape[-1] // 2
    turned = jnp.concatenate([-vectors[..., half_size:], vectors[..., :half_size]], axis=-1)
    return vectors * cosine_table + turned * sine_table


def rotate_back(vectors, cosine_table, sine_table):
    half_size = vectors.shape[-1] // 2
    scaled = vectors * sine_table
    turned = jnp.concatenate([scaled[..., half_size:], -scaled[..., :half_size]], axis=-1)
    return vectors * cosine_table + turned


def angles(position, head_width):
    fractions = jnp.arange(0, head_width, 2).astype(jnp.float32) / head_width
    inverse = jnp.exp(-math.log(10000.0) * fractions)
    phases = position.astype(jnp.float32)[:, None] * inverse[None, :]
    phases = jnp.concatenate([phases, phases], axis=-1)
    return (jnp.cos(phases)[:, None, :], jnp.sin(phases)[:, None, :])


def neighbours(count, step):
    return [(i, i + step) for i in range(count) if 0 <= i + step < count]


def by_shard(term):
    return term.astype(BF).reshape(16, term.shape[0] // 16, term.shape[1])


def gain_rows(gain):
    row = jnp.zeros((8, WIDTH), F32).at[0].set(gain).astype(BF)
    return jnp.broadcast_to(row[None], (16, 8, WIDTH))


def shards(
    tokens, segment_ids, norm1_gain, w_qkv, w_attn_out, norm2_gain, w_in, w_mlp_out, cotangent
):
    row_count = tokens.shape[0]
    model_width = tokens.shape[1]
    hidden_units = w_in.shape[1] // 2
    head_count = HEADS
    head_size = HEAD
    rim_width = HALF
    key_span = row_count + 2 * rim_width
    score_scale = 1.0 / math.sqrt(head_size)
    at = place()
    where = jnp.stack([at["x_high"], at["z"], at["core"]]).astype(jnp.int32)
    shard_place = at["shard"]

    gains = jnp.stack([norm1_gain, norm2_gain])
    spread_gains = lax.dynamic_update_slice(
        jnp.zeros((16, WIDTH), BF), gains, (jnp.zeros((), jnp.int32), shard_place * 48)
    )
    first_piece = jnp.concatenate(
        [w_qkv[:, :WIDTH], w_qkv[:, WIDTH : 2 * WIDTH], w_qkv[:, 2 * WIDTH :], spread_gains]
    )
    second_piece = jnp.concatenate(
        [
            w_attn_out,
            w_in[:, :WIDTH],
            w_in[:, WIDTH : 2 * WIDTH],
            w_in[:, 2 * WIDTH :],
            w_mlp_out,
            jnp.zeros((8, WIDTH), BF),
        ]
    )
    wqkv_all, gain_table = call(
        assemble_first,
        where,
        gather_group(first_piece),
        [((WIDTH, 3 * WIDTH), BF), ((16, WIDTH), F32)],
    )
    first_norm_gains, second_norm_gains = gain_table[0], gain_table[1]
    wout_all, win_all, wdown_all = call(
        assemble_second,
        where,
        gather_group(second_piece),
        [((WIDTH, WIDTH), BF), ((WIDTH, 3 * WIDTH), BF), ((1152, WIDTH), BF)],
    )

    first_row = shard_place * row_count
    seq_segs = segment_ids[0]
    own_segs = lax.dynamic_slice_in_dim(seq_segs, first_row, row_count, 0)
    earlier = jnp.sum((seq_segs[None, :] < own_segs[:, None]).astype(jnp.int32), axis=1)
    position = jnp.arange(row_count, dtype=jnp.int32) + first_row - earlier
    cosine_table, sine_table = angles(position, head_size)
    segs_pad = jnp.pad(seq_segs, (rim_width, rim_width), constant_values=-1)
    key_segs = lax.dynamic_slice_in_dim(segs_pad, first_row, key_span, 0)
    row_index = jnp.arange(row_count, dtype=jnp.int32)[:, None] + rim_width
    column_index = jnp.arange(key_span, dtype=jnp.int32)[None, :]
    allowed = (jnp.abs(row_index - column_index) <= rim_width) & (
        own_segs[:, None] == key_segs[None, :]
    )
    input_rows = tokens.astype(jnp.float32)
    first_standardized, first_inverse_scale = normalize_rows(input_rows)
    first_normalized = (first_standardized * first_norm_gains).astype(jnp.bfloat16)
    qkv_all = jnp.dot(first_normalized, wqkv_all, preferred_element_type=jnp.float32)
    split_parts = qkv_all.reshape(row_count, 3, head_count, head_size)
    queries = rotate(split_parts[:, 0], cosine_table, sine_table).astype(jnp.bfloat16)
    key_rows = rotate(split_parts[:, 1], cosine_table, sine_table).astype(jnp.bfloat16)
    values = split_parts[:, 2].astype(jnp.bfloat16)
    joined = jnp.concatenate(
        [key_rows.reshape(row_count, model_width), values.reshape(row_count, model_width)], axis=1
    )
    joined_ext = jnp.concatenate(
        [
            lax.ppermute(joined[row_count - rim_width :], "shard", neighbours(16, 1)),
            joined,
            lax.ppermute(joined[:rim_width], "shard", neighbours(16, -1)),
        ]
    )
    keys_ext = joined_ext[:, :model_width].reshape(key_span, head_count, head_size)
    values_ext = joined_ext[:, model_width:].reshape(key_span, head_count, head_size)

    def scores_of():
        raw_scores = (
            jnp.einsum("qhd,khd->hqk", queries, keys_ext, preferred_element_type=jnp.float32)
            * score_scale
        )
        return jnp.where(allowed[None], raw_scores, masked_score)

    scores = scores_of()
    row_max = jnp.max(scores, axis=-1, keepdims=True)
    exponent = jnp.exp(scores - row_max)
    row_total = jnp.sum(exponent, axis=-1, keepdims=True)
    log_total = row_max + jnp.log(row_total)
    probs_low = (exponent / row_total).astype(jnp.bfloat16)
    context = jnp.einsum("hqk,khd->qhd", probs_low, values_ext, preferred_element_type=jnp.float32)
    context = context.reshape(row_count, model_width).astype(jnp.bfloat16)
    attn_out = jnp.dot(context, wout_all, preferred_element_type=jnp.float32)
    hidden_rows = input_rows + attn_out
    second_standardized, second_inverse_scale = normalize_rows(hidden_rows)
    second_normalized = (second_standardized * second_norm_gains).astype(jnp.bfloat16)
    gate_up = jnp.dot(second_normalized, win_all, preferred_element_type=jnp.float32)
    gate_part = gate_up[:, :hidden_units]
    up_part = gate_up[:, hidden_units:]
    activated = jax.nn.gelu(gate_part, approximate=False)
    mixed_rows = (activated * up_part).astype(jnp.bfloat16)
    mlp_out = jnp.dot(mixed_rows, wdown_all, preferred_element_type=jnp.float32)
    output = (hidden_rows + mlp_out).astype(jnp.bfloat16)
    grad_out = cotangent.astype(jnp.float32)
    term_down = jnp.einsum("tf,td->fd", mixed_rows, cotangent, preferred_element_type=jnp.float32)
    grad_mixed = jnp.einsum("td,fd->tf", cotangent, wdown_all, preferred_element_type=jnp.float32)
    normal_cdf = 0.5 * (1.0 + lax.erf(gate_part * root_half))
    normal_pdf = jnp.exp(-0.5 * gate_part * gate_part) * density_factor
    grad_gate = grad_mixed * up_part * (normal_cdf + gate_part * normal_pdf)
    grad_up = grad_mixed * activated
    grad_gate_up = jnp.concatenate([grad_gate, grad_up], axis=1).astype(jnp.bfloat16)
    term_in = [
        jnp.einsum(
            "td,tf->df",
            second_normalized,
            grad_gate_up[:, part * WIDTH : (part + 1) * WIDTH],
            preferred_element_type=jnp.float32,
        )
        for part in range(3)
    ]
    second_normalized_gradient = jnp.einsum(
        "tf,df->td", grad_gate_up, win_all, preferred_element_type=jnp.float32
    )
    second_gain_term = jnp.sum(second_normalized_gradient * second_standardized, axis=0)
    hidden_gradient = grad_out + norm_backward_pass(
        second_normalized_gradient * second_norm_gains,
        second_standardized,
        second_inverse_scale,
    )
    mlp_terms = jnp.concatenate(
        [by_shard(term) for term in term_in] + [by_shard(term_down), gain_rows(second_gain_term)],
        axis=1,
    )
    mlp_block = shard_sum(core_sum(mlp_terms, at, 224), at, 112)

    grad_attn = hidden_gradient.astype(jnp.bfloat16)
    term_out = jnp.einsum("td,te->de", context, grad_attn, preferred_element_type=jnp.float32)
    grad_context = jnp.einsum("te,de->td", grad_attn, wout_all, preferred_element_type=jnp.float32)
    grad_context = grad_context.astype(jnp.bfloat16).reshape(row_count, head_count, head_size)
    attn_probs = jnp.exp(scores_of() - log_total)
    probs_again = attn_probs.astype(jnp.bfloat16)
    grad_probs = jnp.einsum(
        "qhd,khd->hqk", grad_context, values_ext, preferred_element_type=jnp.float32
    )
    inner = jnp.sum(attn_probs * grad_probs, axis=-1, keepdims=True)
    grad_scores = (attn_probs * (grad_probs - inner)).astype(jnp.bfloat16)
    grad_queries = (
        jnp.einsum("hqk,khd->qhd", grad_scores, keys_ext, preferred_element_type=jnp.float32)
        * score_scale
    )
    grad_keys_ext = (
        jnp.einsum("hqk,qhd->khd", grad_scores, queries, preferred_element_type=jnp.float32)
        * score_scale
    )
    grad_values_ext = jnp.einsum(
        "hqk,qhd->khd", probs_again, grad_context, preferred_element_type=jnp.float32
    )
    grad_joined = jnp.concatenate(
        [
            grad_keys_ext.reshape(key_span, model_width),
            grad_values_ext.reshape(key_span, model_width),
        ],
        axis=1,
    )
    from_below = lax.ppermute(
        grad_joined[row_count + rim_width :].astype(jnp.bfloat16), "shard", neighbours(16, 1)
    ).astype(jnp.float32)
    from_above = lax.ppermute(
        grad_joined[:rim_width].astype(jnp.bfloat16), "shard", neighbours(16, -1)
    ).astype(jnp.float32)
    own_grads = grad_joined[rim_width : rim_width + row_count]
    own_grads = jnp.concatenate(
        [
            own_grads[:rim_width] + from_below,
            own_grads[rim_width : row_count - rim_width],
            own_grads[row_count - rim_width :] + from_above,
        ]
    )
    grad_keys = own_grads[:, :model_width].reshape(row_count, head_count, head_size)
    grad_values = own_grads[:, model_width:]
    grad_qkv = jnp.concatenate(
        [
            rotate_back(grad_queries, cosine_table, sine_table).reshape(row_count, model_width),
            rotate_back(grad_keys, cosine_table, sine_table).reshape(row_count, model_width),
            grad_values,
        ],
        axis=1,
    ).astype(jnp.bfloat16)
    term_qkv = [
        jnp.einsum(
            "td,te->de",
            first_normalized,
            grad_qkv[:, part * WIDTH : (part + 1) * WIDTH],
            preferred_element_type=jnp.float32,
        )
        for part in range(3)
    ]
    first_normalized_gradient = jnp.einsum(
        "te,de->td", grad_qkv, wqkv_all, preferred_element_type=jnp.float32
    )
    first_gain_term = jnp.sum(first_normalized_gradient * first_standardized, axis=0)
    grad_tokens = (
        hidden_gradient
        + norm_backward_pass(
            first_normalized_gradient * first_norm_gains,
            first_standardized,
            first_inverse_scale,
        )
    ).astype(jnp.bfloat16)
    attn_terms = jnp.concatenate(
        [by_shard(term) for term in term_qkv] + [by_shard(term_out), gain_rows(first_gain_term)],
        axis=1,
    )
    attn_block = shard_sum(core_sum(attn_terms, at, 200), at, 96)
    total = rep_sum(jnp.concatenate([mlp_block, attn_block]), at).astype(F32)

    def own_gain(row):
        return lax.dynamic_slice_in_dim(row, shard_place * 48, 48)

    attn_total = total[224:]
    return (
        output,
        grad_tokens,
        own_gain(attn_total[192]),
        jnp.concatenate([attn_total[0:48], attn_total[48:96], attn_total[96:144]], axis=1),
        attn_total[144:192],
        own_gain(total[216]),
        jnp.concatenate([total[0:48], total[48:96], total[96:144]], axis=1),
        total[144:216],
    )


def solution(mesh):
    return jax.shard_map(
        shards,
        mesh=mesh,
        in_specs=(
            P(("rep", "shard"), None),
            P("rep", None),
            P("shard"),
            P("shard", None),
            P("shard", None),
            P("shard"),
            P("shard", None),
            P("shard", None),
            P(("rep", "shard"), None),
        ),
        out_specs=(
            P(("rep", "shard"), None),
            P(("rep", "shard"), None),
            P("shard"),
            P("shard", None),
            P("shard", None),
            P("shard"),
            P("shard", None),
            P("shard", None),
        ),
        check_vma=False,
    )
```

time: 615 us -> 257 us (0.42)
  waiting for transfers between devices: 401 us -> 73.8 us
  blocking collectives: 96.1 us -> 0 us
  starting transfers between devices: 8.58 us -> 91.2 us
  between operations: 15.9 us -> 2.21 us
  matrix products: 45.8 us -> 33 us
  Pallas kernels: 0 us -> 7.92 us
    reduce_scatter x4 -> x0, waiting for transfers between devices: 185 us -> none  [the longest x1 80.3 us: shards(): lax.psum_scatter(term_in.astype(jnp.bfloat16), 'shard', scatter_dimension...]
    all_gather x4 -> x0, waiting for transfers between devices: 136 us -> none  [the longest x1 51.7 us: shards(): weight_piece = lax.all_gather(w_in, 'shard', axis=0, tiled=True)]
    ppermute x4 -> x59, starting transfers between devices: 8.01 us -> 91.2 us  [the longest x55 74.7 us: send(): return lax.ppermute(value, AXES, route)]
    unnamed x2 -> x0, blocking collectives: 76.5 us -> none
    psum x1 -> x0, waiting for transfers between devices: 76 us -> none  [shards(): lax.psum(attn_parts[1].astype(jnp.bfloat16), 'rep').astype(jnp.float32)]
    ppermute x4 -> x59, waiting for transfers between devices: 0.9 us -> 73.8 us  [the longest x55 73.8 us: send(): return lax.ppermute(value, AXES, route)]
    psum x1 -> x0, blocking collectives: 19.6 us -> none  [shards(): lax.psum(attn_parts[0].astype(jnp.bfloat16), 'rep').astype(jnp.float32)]
    scatter-add x2 -> x0, local copies, waits for them, and re-layouts: 13.2 us -> none  [the longest x1 6.64 us: shards(): own_grads = own_grads.at[:rim_width].add(from_below)]
  transfers between devices with their start and end apart: 13 -> 59, of which waited for: 9 -> 29; matrix products, arithmetic and copies ran while one was open for 12% -> 11% of each run, Pallas kernels for 0% -> 1%
where the time goes in v1:
time: 257 us; the launch traced here: 252 us
  starting transfers between devices  91.2 us (35%)
  waiting for transfers between devices  73.8 us (29%)
  matrix products  33 us (13%)
  local copies, waits for them, and re-layouts  23.9 us (9%)
  other arithmetic  20.1 us (8%)
  Pallas kernels  7.92 us (3%)
    ppermute x55, starting transfers between devices, send(): return lax.ppermute(value, AXES, route)  74.7 us
    ppermute x55, waiting for transfers between devices, send(): return lax.ppermute(value, AXES, route)  73.8 us
    unnamed x116, local copies, waits for them, and re-layouts  12.5 us
    ppermute x1, starting transfers between devices, shards(): lax.ppermute(grad_joined[:rim_width].astype(jnp.bfloat16), 'shard', neigh...  10.1 us
    pallas_call x2, Pallas kernels, call(): pl.pallas_call(kernel, out_shape=[jax.ShapeDtypeStruct(shape, kind) for s...  7.92 us
    convert_element_type x2, other arithmetic, core_sum(): (mine.astype(F32) + arrived.astype(F32)).astype(BF)  5.73 us
  transfers between devices with their start and end apart: 59, of which 29 were waited for; matrix products, arithmetic and copies ran while one was open for 11% of the time, Pallas kernels for 1%

profile of v1, /device:TPU:0, one launch (start us, length us, event | category | flops | bytes accessed | tf_op | source)
XLA Modules:
  0.0 252.2 jit_solution(13838222689946251517)
XLA Ops:
  19.5 4.0 %collective-permute-done.3.refs_4_ = bf16[160,768]{1,0:T(8,128)(2,1)S(1)} collective-permute-done((bf16[160,768]{1,0:T(8,128)(2,1)S(1)}, bf16[160,768]{1,0:T(8,128)(2,1)S(1)}, u32[]{:S(2)}, u32[]{:S(2)}) %collective-permute-start.3) | collective-permute-done | bytes 245792 | tf_op jit(solution)/shard_map/ppermute | solution.py:56
  27.9 3.1 %collective-permute-done.6.refs_7_ = bf16[160,768]{1,0:T(8,128)(2,1)S(1)} collective-permute-done((bf16[160,768]{1,0:T(8,128)(2,1)S(1)}, bf16[160,768]{1,0:T(8,128)(2,1)S(1)}, u32[]{:S(2)}, u32[]{:S(2)}) %collective-permute-start.6) | collective-permute-done | bytes 245792 | tf_op jit(solution)/shard_map/ppermute | solution.py:56
  35.5 3.5 %shard_map.152 = (bf16[768,2304]{1,0:T(8,128)(2,1)}, f32[16,768]{1,0:T(8,128)S(1)}) custom-call(s32[3]{0:T(128)S(1)} %pad_add_fusion.where_ref, bf16[160,768]{1,0:T(8,128)(2,1)S(1)} %pad_maximum_fusion.8.refs_0_, bf16[160,768]{1,0:T(8,128)(2,1)S(1)} %collective-permute-done.refs_1_, bf16[160,768]{1,0:T(8,128)(2,1)S(1)} %collective-permute-done.1.refs_2_, ...), custom_call_target="tpu_custom_call" | custom-call | tf_op jit(solution)/shard_map/pallas_call | solution.py:136
  39.0 3.6 %fusion.100 = f32[256,2304]{0,1:T(8,128)S(1)} fusion(bf16[768,2304]{1,0:T(8,128)(2,1)} %get-tuple-element.38, bf16[256,768]{1,0:T(8,128)(2,1)S(1)} %copy-done.2, f32[768]{0:T(1024)S(1)} %get-tuple-element.49, f32[256]{0:T(256)S(1)} %add_rsqrt_fusion.1, f32[256]{0:T(256)S(1)} %broadcast_multiply_fusion.10), kind=kOutput, calls=%fused_computation.253 | convolution fusion | flops 906952704 | bytes 6296576 | tf_op jit(solution)/shard_map/dot_general | solution.py:301
  45.7 3.1 %collective-permute-start.15 = (bf16[64,1536]{0,1:T(8,128)(2,1)S(1)}, bf16[64,1536]{0,1:T(8,128)(2,1)S(1)}, u32[]{:S(2)}, u32[]{:S(2)}) collective-permute-start(bf16[64,1536]{0,1:T(8,128)(2,1)S(1)} %get-tuple-element.87), channel_id=1, source_target_pairs={{0,1},{1,2},{2,3},{3,4},{4,5},{5,6},{6,7},{7,8},{8,9},{9,10},{10,1... | collective-permute-start | bytes 589832 | tf_op jit(solution)/shard_map/ppermute | solution.py:311
  53.1 6.7 %collective-permute-start.21 = (bf16[272,768]{1,0:T(8,128)(2,1)S(1)}, bf16[272,768]{1,0:T(8,128)(2,1)S(1)}, u32[]{:S(2)}, u32[]{:S(2)}) collective-permute-start(bf16[272,768]{1,0:T(8,128)(2,1)S(1)} %collective-permute-done.17.refs_1_), channel_id=1, source_target_pairs={{0,2},{1,3},{2,4},{3,5},{4,6},{5,7},{6,0},{7,1},{8,10},{9,11},{10,... | collective-permute-start | bytes 1253384 | tf_op jit(solution)/shard_map/ppermute | solution.py:56
  63.3 5.4 %collective-permute-start.23 = (bf16[272,768]{1,0:T(8,128)(2,1)S(1)}, bf16[272,768]{1,0:T(8,128)(2,1)S(1)}, u32[]{:S(2)}, u32[]{:S(2)}) collective-permute-start(bf16[272,768]{1,0:T(8,128)(2,1)S(1)} %collective-permute-done.20.refs_4_), channel_id=1, source_target_pairs={{0,72},{1,73},{2,74},{3,75},{4,76},{5,77},{6,78},{7,79},{8,64},{9,... | collective-permute-start | bytes 1253384 | tf_op jit(solution)/shard_map/ppermute | solution.py:56
  68.7 3.1 %collective-permute-start.26 = (bf16[272,768]{1,0:T(8,128)(2,1)S(1)}, bf16[272,768]{1,0:T(8,128)(2,1)S(1)}, u32[]{:S(2)}, u32[]{:S(2)}) collective-permute-start(bf16[272,768]{1,0:T(8,128)(2,1)S(1)} %collective-permute-done.18.refs_2_), channel_id=1, source_target_pairs={{0,1},{1,0},{2,3},{3,2},{4,5},{5,4},{6,7},{7,6},{8,9},{9,8},{10,11... | collective-permute-start | bytes 1253384 | tf_op jit(solution)/shard_map/ppermute | solution.py:56
  82.9 4.5 %shard_map.153 = (bf16[768,768]{1,0:T(8,128)(2,1)}, bf16[768,2304]{1,0:T(8,128)(2,1)}, bf16[1152,768]{1,0:T(8,128)(2,1)}) custom-call(s32[3]{0:T(128)S(1)} %pad_add_fusion.where_ref, bf16[272,768]{1,0:T(8,128)(2,1)S(1)} %constant_dynamic-update-slice_fusion.refs_0_, bf16[272,768]{1,0:T(8,128)(2,1)S(1)} %collective-permute-done.17.refs_1_, ...), custom_call_target="tpu_custom_call" | custom-call | tf_op jit(solution)/shard_map/pallas_call | solution.py:136
  91.3 4.5 %multiply_convert_fusion.1 = (bf16[256,1152]{1,0:T(8,128)(2,1)S(1)}, f32[256,1152]{1,0:T(8,128)}, bf16[256,1152]{1,0:T(8,128)(2,1)S(1)}) fusion(f32[256,2304]{1,0:T(8,128)S(1)} %fusion.114, bf16[1152,768]{1,0:T(8,128)(2,1)S(1)} %copy-done.16, bf16[256,768]{1,0:T(8,128)(2,1)S(1)} %copy-done.23), kind=kOutput, calls=%fused_computation.72 | convolution fusion | flops 475693056 | bytes 6881280 | tf_op jit(solution)/shard_map/td,fd->tf/dot_general | solution.py:347
  101.4 3.7 %multiply_reduce_fusion = (f32[12,256]{1,0:T(8,128)S(1)}, f32[12,256,384]{2,1,0:T(8,128)S(1)}) fusion(f32[12,256,384]{2,1,0:T(8,128)} %copy-done, f32[12,256]{1,0:T(8,128)S(1)} %log_add_fusion, bf16[256,12,64]{0,2,1:T(8,128)(2,1)S(1)} %bitcast.206, bf16[384,12,64]{0,2,1:T(8,128)(2,1)} %bitcast.212), kind=kOutput, calls=%fused_computation.5 | convolution fusion | flops 154530816 | bytes 10444800 | tf_op jit(solution)/shard_map/qhd,khd->hqk/dot_general | solution.py:383
  116.0 10.1 %collective-permute-start.33 = (bf16[64,1536]{0,1:T(8,128)(2,1)S(1)}, bf16[64,1536]{0,1:T(8,128)(2,1)S(1)}, u32[]{:S(2)}, u32[]{:S(2)}) collective-permute-start(bf16[64,1536]{0,1:T(8,128)(2,1)S(1)} %get-tuple-element.78), channel_id=1, source_target_pairs={{1,0},{2,1},{3,2},{4,3},{5,4},{6,5},{7,6},{8,7},{9,8},{10,9},{11,1... | collective-permute-start | bytes 589832 | tf_op jit(solution)/shard_map/ppermute | solution.py:409
  145.7 3.2 %fusion.1 = bf16[8,200,768]{2,1,0:T(8,128)(2,1)S(1)} fusion(bf16[8,200,768]{2,1,0:T(8,128)(2,1)} %collective-permute-done.43, bf16[8,2,200,768]{3,2,1,0:T(8,128)(2,1)} %copy-done.5, s32[]{:T(128)S(6)} %select_n.162), kind=kLoop, calls=%fused_computation.3 | loop fusion | flops 4915200 | bytes 7372804 | tf_op jit(solution)/shard_map/convert_element_type | solution.py:153
  149.1 8.4 %collective-permute-start.48 = (bf16[4,104,768]{2,1,0:T(8,128)(2,1)S(1)}, bf16[4,104,768]{2,1,0:T(8,128)(2,1)S(1)}, u32[]{:S(2)}, u32[]{:S(2)}) collective-permute-start(bf16[4,104,768]{2,1,0:T(8,128)(2,1)S(1)} %dynamic-slice_bitcast_fusion.3), channel_id=1, source_target_pairs={{0,72},{1,73},{2,74},{3,75},{4,76},{5,77},{6,78},{7,79},{8,64},{9,... | collective-permute-start | bytes 1916936 | tf_op jit(solution)/shard_map/ppermute | solution.py:56
  162.8 6.3 %collective-permute-done.46 = bf16[2,96,768]{2,1,0:T(8,128)(2,1)S(1)} collective-permute-done((bf16[2,96,768]{2,1,0:T(8,128)(2,1)S(1)}, bf16[2,96,768]{2,1,0:T(8,128)(2,1)S(1)}, u32[]{:S(2)}, u32[]{:S(2)}) %collective-permute-start.46) | collective-permute-done | bytes 294944 | tf_op jit(solution)/shard_map/ppermute | solution.py:56
  175.7 7.1 %collective-permute-done.37 = bf16[2,112,768]{2,1,0:T(8,128)(2,1)S(1)} collective-permute-done((bf16[2,112,768]{2,1,0:T(8,128)(2,1)S(1)}, bf16[2,112,768]{2,1,0:T(8,128)(2,1)S(1)}, u32[]{:S(2)}, u32[]{:S(2)}) %collective-permute-start.37) | collective-permute-done | bytes 344096 | tf_op jit(solution)/shard_map/ppermute | solution.py:56
  184.5 4.6 %collective-permute-done.35 = bf16[2,112,768]{2,1,0:T(8,128)(2,1)S(1)} collective-permute-done((bf16[2,112,768]{2,1,0:T(8,128)(2,1)S(1)}, bf16[2,112,768]{2,1,0:T(8,128)(2,1)S(1)}, u32[]{:S(2)}, u32[]{:S(2)}) %collective-permute-start.35) | collective-permute-done | bytes 344096 | tf_op jit(solution)/shard_map/ppermute | solution.py:56
  190.2 6.7 %collective-permute-done.38 = bf16[112,768]{1,0:T(8,128)(2,1)S(1)} collective-permute-done((bf16[112,768]{1,0:T(8,128)(2,1)S(1)}, bf16[112,768]{1,0:T(8,128)(2,1)S(1)}, u32[]{:S(2)}, u32[]{:S(2)}) %collective-permute-start.38) | collective-permute-done | bytes 172064 | tf_op jit(solution)/shard_map/ppermute | solution.py:56
  199.8 3.3 %collective-permute-start.42 = (bf16[112,768]{1,0:T(8,128)(2,1)S(1)}, bf16[112,768]{1,0:T(8,128)(2,1)S(1)}, u32[]{:S(2)}, u32[]{:S(2)}) collective-permute-start(bf16[112,768]{1,0:T(8,128)(2,1)S(1)} %get-tuple-element.95), channel_id=1, source_target_pairs={{0,4},{1,5},{2,6},{3,7},{4,0},{5,1},{6,2},{7,3},{8,12},{9,13},{10,... | collective-permute-start | bytes 516104 | tf_op jit(solution)/shard_map/ppermute | solution.py:56
  206.1 4.0 %collective-permute-done.49 = bf16[104,768]{1,0:T(8,128)(2,1)S(1)} collective-permute-done((bf16[104,768]{1,0:T(8,128)(2,1)S(1)}, bf16[104,768]{1,0:T(8,128)(2,1)S(1)}, u32[]{:S(2)}, u32[]{:S(2)}) %collective-permute-start.49) | collective-permute-done | bytes 159776 | tf_op jit(solution)/shard_map/ppermute | solution.py:56
  217.1 3.3 %collective-permute-start.54 = (bf16[106,768]{1,0:T(8,128)(2,1)S(1)}, bf16[106,768]{1,0:T(8,128)(2,1)S(1)}, u32[]{:S(2)}, u32[]{:S(2)}) collective-permute-start(bf16[106,768]{1,0:T(8,128)(2,1)S(1)} %get-tuple-element.92), channel_id=1, source_target_pairs={{0,32},{1,33},{2,34},{3,35},{4,36},{5,37},{6,38},{7,39},{8,40},{9,... | collective-permute-start | bytes 488456 | tf_op jit(solution)/shard_map/ppermute | solution.py:56
  228.8 5.4 %collective-permute-done.55 = bf16[106,768]{1,0:T(8,128)(2,1)S(1)} collective-permute-done((bf16[106,768]{1,0:T(8,128)(2,1)S(1)}, bf16[106,768]{1,0:T(8,128)(2,1)S(1)}, u32[]{:S(2)}, u32[]{:S(2)}) %collective-permute-start.55) | collective-permute-done | bytes 162848 | tf_op jit(solution)/shard_map/ppermute | solution.py:56
  234.2 3.2 %collective-permute-start.56 = (bf16[106,768]{1,0:T(8,128)(2,1)S(1)}, bf16[106,768]{1,0:T(8,128)(2,1)S(1)}, u32[]{:S(2)}, u32[]{:S(2)}) collective-permute-start(bf16[106,768]{1,0:T(8,128)(2,1)S(1)} %get-tuple-element.51), channel_id=1, source_target_pairs={{0,48},{1,49},{2,50},{3,51},{4,52},{5,53},{6,54},{7,55},{8,56},{9,... | collective-permute-start | bytes 488456 | tf_op jit(solution)/shard_map/ppermute | solution.py:56
  239.8 4.0 %collective-permute-done.56 = bf16[106,768]{1,0:T(8,128)(2,1)S(1)} collective-permute-done((bf16[106,768]{1,0:T(8,128)(2,1)S(1)}, bf16[106,768]{1,0:T(8,128)(2,1)S(1)}, u32[]{:S(2)}, u32[]{:S(2)}) %collective-permute-start.56) | collective-permute-done | bytes 162848 | tf_op jit(solution)/shard_map/ppermute | solution.py:56
  (335 shorter events, 135.3 us)
Async XLA Ops:
  10.0 13.6 %collective-permute-start.3 = (bf16[160,768]{1,0:T(8,128)(2,1)S(1)}, bf16[160,768]{1,0:T(8,128)(2,1)S(1)}, u32[]{:S(2)}, u32[]{:S(2)}) collective-permute-start(bf16[160,768]{1,0:T(8,128)(2,1)S(1)} %pad_maximum_fusion.8.refs_0_), channel_id=1, source_target_pairs={{0,4},{1,5},{2,6},{3,7},{4,0},{5,1},{6,2},{7,3},{8,12},{9,13},{10,... | collective-permute-start | bytes 737288 | tf_op jit(solution)/shard_map/ppermute | solution.py:56
  11.9 12.2 %collective-permute-start.7 = (bf16[160,768]{1,0:T(8,128)(2,1)S(1)}, bf16[160,768]{1,0:T(8,128)(2,1)S(1)}, u32[]{:S(2)}, u32[]{:S(2)}) collective-permute-start(bf16[160,768]{1,0:T(8,128)(2,1)S(1)} %pad_maximum_fusion.8.refs_0_), channel_id=1, source_target_pairs={{0,1},{1,0},{2,3},{3,2},{4,5},{5,4},{6,7},{7,6},{8,9},{9,8},{10,11... | collective-permute-start | bytes 737288 | tf_op jit(solution)/shard_map/ppermute | solution.py:56
  14.7 12.6 %collective-permute-start.4 = (bf16[160,768]{1,0:T(8,128)(2,1)S(1)}, bf16[160,768]{1,0:T(8,128)(2,1)S(1)}, u32[]{:S(2)}, u32[]{:S(2)}) collective-permute-start(bf16[160,768]{1,0:T(8,128)(2,1)S(1)} %collective-permute-done.refs_1_), channel_id=1, source_target_pairs={{0,2},{1,3},{2,4},{3,5},{4,6},{5,7},{6,0},{7,1},{8,10},{9,11},{10,... | collective-permute-start | bytes 737288 | tf_op jit(solution)/shard_map/ppermute | solution.py:56
  31.7 17.3 %collective-permute-start.17 = (bf16[272,768]{1,0:T(8,128)(2,1)S(1)}, bf16[272,768]{1,0:T(8,128)(2,1)S(1)}, u32[]{:S(2)}, u32[]{:S(2)}) collective-permute-start(bf16[272,768]{1,0:T(8,128)(2,1)S(1)} %constant_dynamic-update-slice_fusion.refs_0_), channel_id=1, source_target_pairs={{0,72},{1,73},{2,74},{3,75},{4,76},{5,77},{6,78},{7,79},{8,64},{9,... | collective-permute-start | bytes 1253384 | tf_op jit(solution)/shard_map/ppermute | solution.py:56
  32.3 28.5 %collective-permute-start.18 = (bf16[272,768]{1,0:T(8,128)(2,1)S(1)}, bf16[272,768]{1,0:T(8,128)(2,1)S(1)}, u32[]{:S(2)}, u32[]{:S(2)}) collective-permute-start(bf16[272,768]{1,0:T(8,128)(2,1)S(1)} %constant_dynamic-update-slice_fusion.refs_0_), channel_id=1, source_target_pairs={{0,2},{1,3},{2,4},{3,5},{4,6},{5,7},{6,0},{7,1},{8,10},{9,11},{10,... | collective-permute-start | bytes 1253384 | tf_op jit(solution)/shard_map/ppermute | solution.py:56
  33.7 27.1 %collective-permute-start.19 = (bf16[272,768]{1,0:T(8,128)(2,1)S(1)}, bf16[272,768]{1,0:T(8,128)(2,1)S(1)}, u32[]{:S(2)}, u32[]{:S(2)}) collective-permute-start(bf16[272,768]{1,0:T(8,128)(2,1)S(1)} %constant_dynamic-update-slice_fusion.refs_0_), channel_id=1, source_target_pairs={{0,6},{1,7},{2,0},{3,1},{4,2},{5,3},{6,4},{7,5},{8,14},{9,15},{10,... | collective-permute-start | bytes 1253384 | tf_op jit(solution)/shard_map/ppermute | solution.py:56
  49.0 14.3 %collective-permute-start.20 = (bf16[272,768]{1,0:T(8,128)(2,1)S(1)}, bf16[272,768]{1,0:T(8,128)(2,1)S(1)}, u32[]{:S(2)}, u32[]{:S(2)}) collective-permute-start(bf16[272,768]{1,0:T(8,128)(2,1)S(1)} %constant_dynamic-update-slice_fusion.refs_0_), channel_id=1, source_target_pairs={{0,4},{1,5},{2,6},{3,7},{4,0},{5,1},{6,2},{7,3},{8,12},{9,13},{10,... | collective-permute-start | bytes 1253384 | tf_op jit(solution)/shard_map/ppermute | solution.py:56
  50.1 18.6 %collective-permute-start.24 = (bf16[272,768]{1,0:T(8,128)(2,1)S(1)}, bf16[272,768]{1,0:T(8,128)(2,1)S(1)}, u32[]{:S(2)}, u32[]{:S(2)}) collective-permute-start(bf16[272,768]{1,0:T(8,128)(2,1)S(1)} %constant_dynamic-update-slice_fusion.refs_0_), channel_id=1, source_target_pairs={{0,1},{1,0},{2,3},{3,2},{4,5},{5,4},{6,7},{7,6},{8,9},{9,8},{10,11... | collective-permute-start | bytes 1253384 | tf_op jit(solution)/shard_map/ppermute | solution.py:56
  53.1 21.0 %collective-permute-start.21 = (bf16[272,768]{1,0:T(8,128)(2,1)S(1)}, bf16[272,768]{1,0:T(8,128)(2,1)S(1)}, u32[]{:S(2)}, u32[]{:S(2)}) collective-permute-start(bf16[272,768]{1,0:T(8,128)(2,1)S(1)} %collective-permute-done.17.refs_1_), channel_id=1, source_target_pairs={{0,2},{1,3},{2,4},{3,5},{4,6},{5,7},{6,0},{7,1},{8,10},{9,11},{10,... | collective-permute-start | bytes 1253384 | tf_op jit(solution)/shard_map/ppermute | solution.py:56
  60.7 13.5 %collective-permute-start.22 = (bf16[272,768]{1,0:T(8,128)(2,1)S(1)}, bf16[272,768]{1,0:T(8,128)(2,1)S(1)}, u32[]{:S(2)}, u32[]{:S(2)}) collective-permute-start(bf16[272,768]{1,0:T(8,128)(2,1)S(1)} %collective-permute-done.17.refs_1_), channel_id=1, source_target_pairs={{0,6},{1,7},{2,0},{3,1},{4,2},{5,3},{6,4},{7,5},{8,14},{9,15},{10,... | collective-permute-start | bytes 1253384 | tf_op jit(solution)/shard_map/ppermute | solution.py:56
  60.8 18.2 %collective-permute-start.25 = (bf16[272,768]{1,0:T(8,128)(2,1)S(1)}, bf16[272,768]{1,0:T(8,128)(2,1)S(1)}, u32[]{:S(2)}, u32[]{:S(2)}) collective-permute-start(bf16[272,768]{1,0:T(8,128)(2,1)S(1)} %collective-permute-done.17.refs_1_), channel_id=1, source_target_pairs={{0,1},{1,0},{2,3},{3,2},{4,5},{5,4},{6,7},{7,6},{8,9},{9,8},{10,11... | collective-permute-start | bytes 1253384 | tf_op jit(solution)/shard_map/ppermute | solution.py:56
  63.3 13.2 %collective-permute-start.23 = (bf16[272,768]{1,0:T(8,128)(2,1)S(1)}, bf16[272,768]{1,0:T(8,128)(2,1)S(1)}, u32[]{:S(2)}, u32[]{:S(2)}) collective-permute-start(bf16[272,768]{1,0:T(8,128)(2,1)S(1)} %collective-permute-done.20.refs_4_), channel_id=1, source_target_pairs={{0,72},{1,73},{2,74},{3,75},{4,76},{5,77},{6,78},{7,79},{8,64},{9,... | collective-permute-start | bytes 1253384 | tf_op jit(solution)/shard_map/ppermute | solution.py:56
  114.0 17.5 %collective-permute-start.32 = (bf16[64,1536]{0,1:T(8,128)(2,1)S(1)}, bf16[64,1536]{0,1:T(8,128)(2,1)S(1)}, u32[]{:S(2)}, u32[]{:S(2)}) collective-permute-start(bf16[64,1536]{0,1:T(8,128)(2,1)S(1)} %get-tuple-element.77), channel_id=1, source_target_pairs={{0,1},{1,2},{2,3},{3,4},{4,5},{5,6},{6,7},{7,8},{8,9},{9,10},{10,1... | collective-permute-start | bytes 589832 | tf_op jit(solution)/shard_map/ppermute | solution.py:406
  116.0 15.5 %collective-permute-start.33 = (bf16[64,1536]{0,1:T(8,128)(2,1)S(1)}, bf16[64,1536]{0,1:T(8,128)(2,1)S(1)}, u32[]{:S(2)}, u32[]{:S(2)}) collective-permute-start(bf16[64,1536]{0,1:T(8,128)(2,1)S(1)} %get-tuple-element.78), channel_id=1, source_target_pairs={{1,0},{2,1},{3,2},{4,3},{5,4},{6,5},{7,6},{8,7},{9,8},{10,9},{11,1... | collective-permute-start | bytes 589832 | tf_op jit(solution)/shard_map/ppermute | solution.py:409
  144.3 15.5 %collective-permute-start.34 = (bf16[8,224,768]{2,1,0:T(8,128)(2,1)}, bf16[8,224,768]{2,1,0:T(8,128)(2,1)}, u32[]{:S(2)}, u32[]{:S(2)}) collective-permute-start(bf16[8,224,768]{2,1,0:T(8,128)(2,1)} %dynamic-slice_bitcast_fusion), channel_id=1, source_target_pairs={{0,1},{1,0},{2,3},{3,2},{4,5},{5,4},{6,7},{7,6},{8,9},{9,8},{10,11... | collective-permute-start | bytes 8257544 | tf_op jit(solution)/shard_map/ppermute | solution.py:56
  149.1 47.8 %collective-permute-start.48 = (bf16[4,104,768]{2,1,0:T(8,128)(2,1)S(1)}, bf16[4,104,768]{2,1,0:T(8,128)(2,1)S(1)}, u32[]{:S(2)}, u32[]{:S(2)}) collective-permute-start(bf16[4,104,768]{2,1,0:T(8,128)(2,1)S(1)} %dynamic-slice_bitcast_fusion.3), channel_id=1, source_target_pairs={{0,72},{1,73},{2,74},{3,75},{4,76},{5,77},{6,78},{7,79},{8,64},{9,... | collective-permute-start | bytes 1916936 | tf_op jit(solution)/shard_map/ppermute | solution.py:56
  157.7 12.5 %collective-permute-start.45 = (bf16[2,96,768]{2,1,0:T(8,128)(2,1)S(1)}, bf16[2,96,768]{2,1,0:T(8,128)(2,1)S(1)}, u32[]{:S(2)}, u32[]{:S(2)}) collective-permute-start(bf16[2,96,768]{2,1,0:T(8,128)(2,1)S(1)} %get-tuple-element.76), channel_id=1, source_target_pairs={{0,6},{1,7},{2,0},{3,1},{4,2},{5,3},{6,4},{7,5},{8,14},{9,15},{10,... | collective-permute-start | bytes 884744 | tf_op jit(solution)/shard_map/ppermute | solution.py:56
  157.8 17.6 %collective-permute-start.44 = (bf16[2,96,768]{2,1,0:T(8,128)(2,1)S(1)}, bf16[2,96,768]{2,1,0:T(8,128)(2,1)S(1)}, u32[]{:S(2)}, u32[]{:S(2)}) collective-permute-start(bf16[2,96,768]{2,1,0:T(8,128)(2,1)S(1)} %get-tuple-element.74), channel_id=1, source_target_pairs={{0,2},{1,3},{2,4},{3,5},{4,6},{5,7},{6,0},{7,1},{8,10},{9,11},{10,... | collective-permute-start | bytes 884744 | tf_op jit(solution)/shard_map/ppermute | solution.py:56
  162.6 36.9 %collective-permute-start.39 = (bf16[4,112,768]{2,1,0:T(8,128)(2,1)S(1)}, bf16[4,112,768]{2,1,0:T(8,128)(2,1)S(1)}, u32[]{:S(2)}, u32[]{:S(2)}) collective-permute-start(bf16[4,112,768]{2,1,0:T(8,128)(2,1)S(1)} %dynamic-slice_bitcast_fusion.2), channel_id=1, source_target_pairs={{0,72},{1,73},{2,74},{3,75},{4,76},{5,77},{6,78},{7,79},{8,64},{9,... | collective-permute-start | bytes 2064392 | tf_op jit(solution)/shard_map/ppermute | solution.py:56
  169.1 13.7 %collective-permute-start.37 = (bf16[2,112,768]{2,1,0:T(8,128)(2,1)S(1)}, bf16[2,112,768]{2,1,0:T(8,128)(2,1)S(1)}, u32[]{:S(2)}, u32[]{:S(2)}) collective-permute-start(bf16[2,112,768]{2,1,0:T(8,128)(2,1)S(1)} %get-tuple-element.63), channel_id=1, source_target_pairs={{0,4},{1,5},{2,6},{3,7},{4,0},{5,1},{6,2},{7,3},{8,12},{9,13},{10,... | collective-permute-start | bytes 1032200 | tf_op jit(solution)/shard_map/ppermute | solution.py:56
  170.2 14.2 %collective-permute-start.36 = (bf16[2,112,768]{2,1,0:T(8,128)(2,1)S(1)}, bf16[2,112,768]{2,1,0:T(8,128)(2,1)S(1)}, u32[]{:S(2)}, u32[]{:S(2)}) collective-permute-start(bf16[2,112,768]{2,1,0:T(8,128)(2,1)S(1)} %get-tuple-element.64), channel_id=1, source_target_pairs={{0,6},{1,7},{2,0},{3,1},{4,2},{5,3},{6,4},{7,5},{8,14},{9,15},{10,... | collective-permute-start | bytes 1032200 | tf_op jit(solution)/shard_map/ppermute | solution.py:56
  175.3 13.7 %collective-permute-start.35 = (bf16[2,112,768]{2,1,0:T(8,128)(2,1)S(1)}, bf16[2,112,768]{2,1,0:T(8,128)(2,1)S(1)}, u32[]{:S(2)}, u32[]{:S(2)}) collective-permute-start(bf16[2,112,768]{2,1,0:T(8,128)(2,1)S(1)} %get-tuple-element.62), channel_id=1, source_target_pairs={{0,2},{1,3},{2,4},{3,5},{4,6},{5,7},{6,0},{7,1},{8,10},{9,11},{10,... | collective-permute-start | bytes 1032200 | tf_op jit(solution)/shard_map/ppermute | solution.py:56
  198.0 12.1 %collective-permute-start.49 = (bf16[104,768]{1,0:T(8,128)(2,1)S(1)}, bf16[104,768]{1,0:T(8,128)(2,1)S(1)}, u32[]{:S(2)}, u32[]{:S(2)}) collective-permute-start(bf16[104,768]{1,0:T(8,128)(2,1)S(1)} %get-tuple-element.97), channel_id=1, source_target_pairs={{0,2},{1,3},{2,4},{3,5},{4,6},{5,7},{6,0},{7,1},{8,10},{9,11},{10,... | collective-permute-start | bytes 479240 | tf_op jit(solution)/shard_map/ppermute | solution.py:56
  199.8 13.1 %collective-permute-start.42 = (bf16[112,768]{1,0:T(8,128)(2,1)S(1)}, bf16[112,768]{1,0:T(8,128)(2,1)S(1)}, u32[]{:S(2)}, u32[]{:S(2)}) collective-permute-start(bf16[112,768]{1,0:T(8,128)(2,1)S(1)} %get-tuple-element.95), channel_id=1, source_target_pairs={{0,4},{1,5},{2,6},{3,7},{4,0},{5,1},{6,2},{7,3},{8,12},{9,13},{10,... | collective-permute-start | bytes 516104 | tf_op jit(solution)/shard_map/ppermute | solution.py:56
  (84 other events, 567.4 us)
